TPU v7x, 128 devices: a whole 4x4x4 slice. The times are simulated.
128 devices in a mesh: row: 8 (over z, x_lo), col: 16 (over x_hi, y, core).
Axes of the slice: x: 4 (x_hi: 2, x_lo: 2; x = x_hi * 2 + x_lo), y: 4, z: 4, core: 2. Of those that a mesh axis runs over, the one named last changes fastest.
Arguments:
- points_gen: bfloat16 [24576, 128], P(('row', 'col')), may hold values from -6 to 6
- points_obs: bfloat16 [16384, 128], P(('col', 'row')), may hold values from -6 to 6
- log_mass_gen: float32 [24576], P('row'), may hold values from -1 to 1
- log_mass_obs: float32 [16384], P('col'), may hold values from -1 to 1
Outputs:
- potential_gen: float32 [24576], P('row')
- potential_obs: float32 [16384], P('col')
- costate: float32 [24576, 128], P(('row', 'col'))
All inputs are finite; a program needn't handle non-finite values.
Results may differ from a plain program's by a relative error of at most 0.0015.
Values may be sent and summed in bfloat16 or wider, within the bound.
No kernel may reach another device: no remote copies, remote signals or barrier semaphores. Data moves between devices by JAX's collectives and lax.ppermute only.
A program may use at most 64 MiB of HBM per device.

v0:
```python
import jax
import jax.numpy as jnp
from jax import lax
from jax.sharding import PartitionSpec as P

ITERS = 4


def row_stats(row_scores):
    top = lax.pmax(jnp.max(row_scores, axis=1), "col")
    total = lax.psum(jnp.sum(jnp.exp(row_scores - top[:, None]), axis=1), "col")
    return (top, total)


def col_stats(col_scores):
    top = lax.pmax(jnp.max(col_scores, axis=0), "row")
    total = lax.psum(jnp.sum(jnp.exp(col_scores - top[None, :]), axis=0), "row")
    return (top, total)


def body(points_gen, points_obs, log_mass_gen, log_mass_obs):
    gen_block = lax.all_gather(points_gen, "col", axis=0, tiled=True)
    obs_block = lax.all_gather(points_obs, "row", axis=0, tiled=True)
    temper = gen_block.shape[1] / 64.0
    gen_wide = gen_block.astype(jnp.float32)
    obs_wide = obs_block.astype(jnp.float32)
    gen_sq = jnp.sum(gen_wide * gen_wide, axis=1)
    obs_sq = jnp.sum(obs_wide * obs_wide, axis=1)
    inner_prod = jnp.dot(gen_block, obs_block.T, preferred_element_type=jnp.float32)
    cost_tile = gen_sq[:, None] + obs_sq[None, :] - 2.0 * inner_prod
    potential_gen = jnp.zeros(log_mass_gen.shape, jnp.float32)
    potential_obs = jnp.zeros(log_mass_obs.shape, jnp.float32)
    row_scores = None
    top = None
    total = None
    for step in range(ITERS):
        col_scores = log_mass_gen[:, None] + (potential_gen[:, None] - cost_tile) / temper
        col_top, col_total = col_stats(col_scores)
        potential_obs = temper * (log_mass_obs - col_top - jnp.log(col_total))
        row_scores = log_mass_obs[None, :] + (potential_obs[None, :] - cost_tile) / temper
        top, total = row_stats(row_scores)
        potential_gen = temper * (log_mass_gen - top - jnp.log(total))
    share_rows = points_gen.shape[0]
    first_own = lax.axis_index("col") * share_rows
    weights = jnp.exp(row_scores - top[:, None]).astype(jnp.bfloat16)
    own_total = lax.dynamic_slice_in_dim(total, first_own, share_rows, 0)
    numerator = lax.psum_scatter(
        jnp.dot(weights, obs_block, preferred_element_type=jnp.float32),
        "col",
        scatter_dimension=0,
        tiled=True,
    )
    costate = points_gen.astype(jnp.float32) - numerator / own_total[:, None]
    return (potential_gen, potential_obs, costate)


def solution(mesh):
    return jax.shard_map(
        body,
        mesh=mesh,
        in_specs=(P(("row", "col"), None), P(("col", "row"), None), P("row"), P("col")),
        out_specs=(P("row"), P("col"), P(("row", "col"), None)),
        check_vma=False,
    )
```

profile of v0, /device:TPU:0, one launch (start us, length us, event | category | flops | bytes accessed | tf_op | source)
XLA Modules:
  0.0 842.5 jit_solution(8780058148321684720)
XLA Ops:
  7.2 30.4 %all_gather.7 = bf16[1024,128]{1,0:T(8,128)(2,1)S(1)} all-gather(bf16[128,128]{1,0:T(8,128)(2,1)} %param.5), channel_id=1, replica_groups=mesh['row'=8,'col'=16] {'row'}, dimensions={0}, use_global_device_ids=true | all-gather | bytes 294912 | tf_op jit(solution)/shard_map/all_gather | solution.py:23
  37.8 26.8 %all_gather.6 = bf16[3072,128]{1,0:T(8,128)(2,1)S(1)} all-gather(bf16[192,128]{1,0:T(8,128)(2,1)} %param.4), channel_id=1, replica_groups=mesh['row'=8,'col'=16] {'col'}, dimensions={0}, use_global_device_ids=true | all-gather | bytes 835584 | tf_op jit(solution)/shard_map/all_gather | solution.py:22
  65.1 6.9 fusion.2
  72.0 18.8 %pmax.56 = f32[1024]{0:T(1024)S(1)} all-reduce(f32[1024]{0:T(1024)S(1)} %get-tuple-element.3), channel_id=1, replica_groups=mesh['row'=8,'col'=16] {'row'}, use_global_device_ids=true, to_apply=%region_3.0 | all-reduce | flops 1024 | bytes 8192 | tf_op jit(solution)/shard_map/pmax | solution.py:16
  90.9 6.4 exponential_reduce_fusion.6
  97.3 16.0 %psum.56 = f32[1024]{0:T(1024)S(1)} all-reduce(f32[1024]{0:T(1024)S(1)} %exponential_reduce_fusion.6), channel_id=1, replica_groups=mesh['row'=8,'col'=16] {'row'}, use_global_device_ids=true, to_apply=%region_5.0 | all-reduce | flops 1024 | bytes 8192 | tf_op jit(solution)/shard_map/psum | solution.py:17
  113.4 6.3 fusion.3
  119.7 64.9 %pmax.57 = f32[3072]{0:T(1024)S(1)} all-reduce(f32[3072]{0:T(1024)S(1)} %fusion.3), channel_id=1, replica_groups=mesh['row'=8,'col'=16] {'col'}, use_global_device_ids=true, to_apply=%region_7.0 | all-reduce | flops 3072 | bytes 24576 | tf_op jit(solution)/shard_map/pmax | solution.py:10
  184.6 6.6 exponential_reduce_fusion.5
  191.3 64.9 %psum.57 = f32[3072]{0:T(1024)S(1)} all-reduce(f32[3072]{0:T(1024)S(1)} %exponential_reduce_fusion.5), channel_id=1, replica_groups=mesh['row'=8,'col'=16] {'col'}, use_global_device_ids=true, to_apply=%region_9.0 | all-reduce | flops 3072 | bytes 24576 | tf_op jit(solution)/shard_map/psum | solution.py:11
  262.0 18.1 %pmax.58 = f32[1024]{0:T(1024)S(1)} all-reduce(f32[1024]{0:T(1024)S(1)} %fusion.4), channel_id=1, replica_groups=mesh['row'=8,'col'=16] {'row'}, use_global_device_ids=true, to_apply=%region_11.0 | all-reduce | flops 1024 | bytes 8192 | tf_op jit(solution)/shard_map/pmax | solution.py:16
  280.1 6.5 exponential_reduce_fusion.4
  286.6 16.0 %psum.58 = f32[1024]{0:T(1024)S(1)} all-reduce(f32[1024]{0:T(1024)S(1)} %exponential_reduce_fusion.4), channel_id=1, replica_groups=mesh['row'=8,'col'=16] {'row'}, use_global_device_ids=true, to_apply=%region_13.0 | all-reduce | flops 1024 | bytes 8192 | tf_op jit(solution)/shard_map/psum | solution.py:17
  302.6 6.3 fusion.5
  309.0 65.1 %pmax.59 = f32[3072]{0:T(1024)S(1)} all-reduce(f32[3072]{0:T(1024)S(1)} %fusion.5), channel_id=1, replica_groups=mesh['row'=8,'col'=16] {'col'}, use_global_device_ids=true, to_apply=%region_15.0 | all-reduce | flops 3072 | bytes 24576 | tf_op jit(solution)/shard_map/pmax | solution.py:10
  374.1 6.6 exponential_reduce_fusion.3
  380.7 64.9 %psum.59 = f32[3072]{0:T(1024)S(1)} all-reduce(f32[3072]{0:T(1024)S(1)} %exponential_reduce_fusion.3), channel_id=1, replica_groups=mesh['row'=8,'col'=16] {'col'}, use_global_device_ids=true, to_apply=%region_17.0 | all-reduce | flops 3072 | bytes 24576 | tf_op jit(solution)/shard_map/psum | solution.py:11
  451.5 18.1 %pmax.60 = f32[1024]{0:T(1024)S(1)} all-reduce(f32[1024]{0:T(1024)S(1)} %fusion.6), channel_id=1, replica_groups=mesh['row'=8,'col'=16] {'row'}, use_global_device_ids=true, to_apply=%region_19.0 | all-reduce | flops 1024 | bytes 8192 | tf_op jit(solution)/shard_map/pmax | solution.py:16
  469.5 6.5 exponential_reduce_fusion.2
  476.0 16.0 %psum.60 = f32[1024]{0:T(1024)S(1)} all-reduce(f32[1024]{0:T(1024)S(1)} %exponential_reduce_fusion.2), channel_id=1, replica_groups=mesh['row'=8,'col'=16] {'row'}, use_global_device_ids=true, to_apply=%region_21.0 | all-reduce | flops 1024 | bytes 8192 | tf_op jit(solution)/shard_map/psum | solution.py:17
  492.1 6.3 fusion.7
  498.4 64.9 %pmax.61 = f32[3072]{0:T(1024)S(1)} all-reduce(f32[3072]{0:T(1024)S(1)} %fusion.7), channel_id=1, replica_groups=mesh['row'=8,'col'=16] {'col'}, use_global_device_ids=true, to_apply=%region_23.0 | all-reduce | flops 3072 | bytes 24576 | tf_op jit(solution)/shard_map/pmax | solution.py:10
  563.3 6.6 exponential_reduce_fusion.1
  570.0 64.9 %psum.61 = f32[3072]{0:T(1024)S(1)} all-reduce(f32[3072]{0:T(1024)S(1)} %exponential_reduce_fusion.1), channel_id=1, replica_groups=mesh['row'=8,'col'=16] {'col'}, use_global_device_ids=true, to_apply=%region_25.0 | all-reduce | flops 3072 | bytes 24576 | tf_op jit(solution)/shard_map/psum | solution.py:11
  640.7 18.1 %pmax.62 = f32[1024]{0:T(1024)S(1)} all-reduce(f32[1024]{0:T(1024)S(1)} %fusion.8), channel_id=1, replica_groups=mesh['row'=8,'col'=16] {'row'}, use_global_device_ids=true, to_apply=%region_27.0 | all-reduce | flops 1024 | bytes 8192 | tf_op jit(solution)/shard_map/pmax | solution.py:16
  658.8 6.5 exponential_reduce_fusion
  665.3 16.0 %psum.62 = f32[1024]{0:T(1024)S(1)} all-reduce(f32[1024]{0:T(1024)S(1)} %exponential_reduce_fusion), channel_id=1, replica_groups=mesh['row'=8,'col'=16] {'row'}, use_global_device_ids=true, to_apply=%region_29.0 | all-reduce | flops 1024 | bytes 8192 | tf_op jit(solution)/shard_map/psum | solution.py:17
  681.4 6.3 fusion.9
  687.7 65.2 %pmax.63 = f32[3072]{0:T(1024)S(1)} all-reduce(f32[3072]{0:T(1024)S(1)} %fusion.9), channel_id=1, replica_groups=mesh['row'=8,'col'=16] {'col'}, use_global_device_ids=true, to_apply=%region_31.0 | all-reduce | flops 3072 | bytes 24576 | tf_op jit(solution)/shard_map/pmax | solution.py:10
  752.8 8.8 %fusion.10 = f32[3072,128]{1,0:T(8,128)} fusion(bf16[1024,128]{1,0:T(8,128)(2,1)S(1)} %all_gather.7, f32[3072,1024]{1,0:T(8,128)} %get-tuple-element.4, f32[3072]{0:T(1024)S(1)} %pmax.63, f32[1024]{0:T(1024)S(1)} %subtract_multiply_fusion.4, f32[1024]{0:T(1024)S(1)} %copy-done.1), kind=kOutput, calls=%fused_computation.27 | convolution fusion | flops 821035008 | bytes 14438400 | tf_op jit(solution)/shard_map/dot_general | solution.py:48
  761.6 6.7 fusion.1
  768.3 65.0 %psum.63 = f32[3072]{0:T(1024)S(1)} all-reduce(f32[3072]{0:T(1024)S(1)} %fusion.1), channel_id=1, replica_groups=mesh['row'=8,'col'=16] {'col'}, use_global_device_ids=true, to_apply=%region_33.0 | all-reduce | flops 3072 | bytes 24576 | tf_op jit(solution)/shard_map/psum | solution.py:11
  (26 shorter events, 20.5 us)
Async XLA Ops:
  7.2 826.9 %reduce-scatter.2.cloned.1.call-start = ((), (), s32[]{:S(2)}) async-start(), calls=%async_computation.1 | async-start | bytes 1671168 | tf_op jit(solution)/shard_map/reduce_scatter | solution.py:47
  65.1 25.8 %copy-start = (f32[3072]{0:T(1024)S(1)}, f32[3072]{0:T(1024)}, u32[]{:S(2)}) copy-start(f32[3072]{0:T(1024)} %param.6) | copy-start | bytes 36868
  72.0 41.4 %copy-start.1 = (f32[1024]{0:T(1024)S(1)}, f32[1024]{0:T(1024)}, u32[]{:S(2)}) copy-start(f32[1024]{0:T(1024)} %param.7) | copy-start | bytes 12292
  681.3 80.3 %copy-start.3 = (f32[1024]{0:T(1024)}, f32[1024]{0:T(1024)S(1)}, u32[]{:S(2)}) copy-start(f32[1024]{0:T(1024)S(1)} %subtract_multiply_fusion.4) | copy-start | bytes 12292
  761.6 72.5 %copy-start.2 = (bf16[192,128]{1,0:T(8,128)(2,1)S(1)}, bf16[192,128]{1,0:T(8,128)(2,1)}, u32[]{:S(2)}) copy-start(bf16[192,128]{1,0:T(8,128)(2,1)} %param.4) | copy-start | bytes 147460
Sparse Core Ops, SparseCore 0:
  761.7 65.2 reduce-scatter.1
where the time goes:
time: 844 us; the launch traced here: 843 us
  blocking collectives  714 us (85%)
  other arithmetic  98.2 us (12%)
  matrix products  15.7 us (2%)
  between operations  14.2 us (2%)
    pmax x4, blocking collectives, row_stats(): top = lax.pmax(jnp.max(row_scores, axis=1), 'col')  260 us
    psum x4, blocking collectives, row_stats(): total = lax.psum(jnp.sum(jnp.exp(row_scores - top[:, None]), axis=1), 'col')  260 us
    pmax x4, blocking collectives, col_stats(): top = lax.pmax(jnp.max(col_scores, axis=0), 'row')  73 us
    psum x4, blocking collectives, col_stats(): total = lax.psum(jnp.sum(jnp.exp(col_scores - top[None, :]), axis=0), 'row')  64.2 us
    all_gather x1, blocking collectives, body(): obs_block = lax.all_gather(points_obs, 'row', axis=0, tiled=True)  30.4 us
    all_gather x1, blocking collectives, body(): gen_block = lax.all_gather(points_gen, 'col', axis=0, tiled=True)  26.8 us
    reduce_sum x4, other arithmetic, row_stats(): total = lax.psum(jnp.sum(jnp.exp(row_scores - top[:, None]), axis=1), 'col')  26.6 us
    reduce_sum x4, other arithmetic, col_stats(): total = lax.psum(jnp.sum(jnp.exp(col_scores - top[None, :]), axis=0), 'row')  26 us
  transfers between devices with their start and end apart: 1, of which 0 were waited for; matrix products, arithmetic and copies ran while one was open for 1% of the time, Pallas kernels for 0%

commit v1 on v0

v1 whole, which is shorter than its diff:
```python
import functools
import math

import jax
import jax.numpy as jnp
from jax import lax
from jax.experimental import pallas as pl
from jax.experimental.pallas import tpu as pltpu
from jax.sharding import PartitionSpec as P

ITERS = 4
LANES = 128
CHUNK = 256
SAMPLE = 256
LOW, HIGH = 1e-20, 1e30
STEEP, FAINT, NOTHING = 20.0, 60.0, 60.0
VMEM = pl.BlockSpec(memory_space=pltpu.VMEM)
SMEM = pl.BlockSpec(memory_space=pltpu.SMEM)
NT = (((1,), (1,)), ((), ()))


def lse_over(parts):
    top = functools.reduce(jnp.maximum, parts)
    return top + jnp.log(sum(jnp.exp(part - top) for part in parts))


def planes(ref):
    return [ref[k] for k in range(ref.shape[0])]


def scores(left, right, left_wide):
    prod = lax.dot_general(left, right, NT, preferred_element_type=jnp.float32)
    return prod + jnp.concatenate([left_wide] * (right.shape[0] // LANES), axis=1)


def fold(values, op):
    rows, width = values.shape
    return op(values.reshape(rows // 8, 8, width), axis=0)


def store_row(ref, first, row):
    for part in range(row.shape[1] // LANES):
        ref[pl.ds(first + part, 1), :] = row[:, part * LANES : (part + 1) * LANES]


def dense_of(row):
    return jnp.concatenate([row[:, k * LANES : (k + 1) * LANES] for k in range(row.shape[1] // LANES)], axis=0)


def row_of(dense):
    return jnp.concatenate([dense[k : k + 1, :] for k in range(dense.shape[0])], axis=1)


def widen(dense, wide_ref):
    for part in range(dense.shape[0]):
        row = jnp.broadcast_to(dense[part : part + 1, :], (LANES, LANES))
        wide_ref[part * LANES : (part + 1) * LANES, :] = jnp.transpose(row)


def squares(points):
    wide = points.astype(jnp.float32)
    square = wide * wide
    high = square.astype(jnp.bfloat16)
    low = (square - high.astype(jnp.float32)).astype(jnp.bfloat16)
    ones = jnp.ones((8, LANES), jnp.bfloat16)
    row = lax.dot_general(ones, high, NT, preferred_element_type=jnp.float32)
    row += lax.dot_general(ones, low, NT, preferred_element_type=jnp.float32)
    return dense_of(row[:1, :])


def in_parts(row):
    high = row.astype(jnp.bfloat16).astype(jnp.float32)
    middle = (row - high).astype(jnp.bfloat16).astype(jnp.float32)
    low = row - high - middle
    line = lax.broadcasted_iota(jnp.int32, (16, row.shape[1]), 0)
    parts = jnp.where(line == 0, high, jnp.where(line == 1, middle, jnp.where(line == 2, low, 0.0)))
    return parts.astype(jnp.bfloat16)


def means_of(left_ref, chunk, values, mean_ref):
    left_t = jnp.transpose(left_ref[...].astype(jnp.float32))
    left_t = jnp.concatenate([left_t, jnp.ones((16, left_t.shape[1]), jnp.float32)], axis=0).astype(jnp.bfloat16)
    numer = jnp.dot(left_t, values.astype(jnp.bfloat16), preferred_element_type=jnp.float32)
    mean = numer[:LANES, :] / numer[LANES : LANES + 1, :]
    mean_ref[pl.ds(pl.multiple_of(chunk * CHUNK, CHUNK), CHUNK), :] = jnp.transpose(mean)


def exact_pass(left_ref, right_ref, wide_ref, shift_ref, total_ref, mean_ref=None):
    n, m = left_ref.shape[0], right_ref.shape[0]
    block = 512
    per = CHUNK // LANES

    def one(chunk, carry):
        right = right_ref[pl.ds(pl.multiple_of(chunk * CHUNK, CHUNK), CHUNK), :]

        def largest(step, top):
            rows = pl.ds(pl.multiple_of(step * block, block), block)
            return jnp.maximum(top, fold(scores(left_ref[rows, :], right, wide_ref[rows, :]), jnp.max))

        top = lax.fori_loop(0, n // block, largest, jnp.full((8, CHUNK), -3e38, jnp.float32))
        top = jnp.max(top, axis=0, keepdims=True)

        def add(step, total):
            rows = pl.ds(pl.multiple_of(step * block, block), block)
            return total + fold(jnp.exp(scores(left_ref[rows, :], right, wide_ref[rows, :]) - top), jnp.sum)

        total = lax.fori_loop(0, n // block, add, jnp.zeros((8, CHUNK), jnp.float32))
        store_row(shift_ref, chunk * per, top)
        store_row(total_ref, chunk * per, jnp.sum(total, axis=0, keepdims=True))
        if mean_ref is not None:
            means_of(left_ref, chunk, jnp.exp(scores(left_ref[...], right, wide_ref[...]) - top), mean_ref)
        return carry

    lax.fori_loop(0, m // CHUNK, one, 0)


def sampled_pass(left_ref, right_ref, wide_ref, shift_ref, total_ref, matrix_ref=None):
    m = right_ref.shape[0]
    per = CHUNK // LANES
    for chunk in range(m // CHUNK):
        right = right_ref[chunk * CHUNK : (chunk + 1) * CHUNK, :]
        some = scores(left_ref[:SAMPLE, :], right, wide_ref[:SAMPLE, :])
        shift = jnp.max(fold(some, jnp.max), axis=0, keepdims=True)
        values = jnp.exp(scores(left_ref[...], right, wide_ref[...]) - shift)
        total = jnp.sum(fold(values, jnp.sum), axis=0, keepdims=True)
        store_row(shift_ref, chunk * per, shift)
        store_row(total_ref, chunk * per, total)
        if matrix_ref is not None:
            matrix_ref[:, chunk * CHUNK : (chunk + 1) * CHUNK] = values.astype(jnp.bfloat16)

    @pl.when(jnp.logical_not(jnp.max(total_ref[...]) < HIGH))
    def _():
        exact_pass(left_ref, right_ref, wide_ref, shift_ref, total_ref)
        if matrix_ref is not None:
            for chunk in range(m // CHUNK):
                across = pl.ds(chunk * CHUNK, CHUNK)
                top = row_of(shift_ref[chunk * per : (chunk + 1) * per, :])
                values = jnp.exp(scores(left_ref[...], right_ref[across, :], wide_ref[...]) - top)
                matrix_ref[:, across] = values.astype(jnp.bfloat16)

    return shift_ref[...] + jnp.log(total_ref[...])


def spread(out_ref, value):
    for copy in range(out_ref.shape[0]):
        out_ref[copy] = value


def first_kernel(
    core_ref, same_ref, other_ref, right_ref, mass_ref,
    out_ref, left_ref, sq_ref, right_sq_ref, wide_ref, shift_ref, total_ref,
):
    core = core_ref[0]
    right_sq_ref[...] = squares(right_ref[...])
    count, own, _ = same_ref.shape
    for k in range(count):
        left_ref[pl.ds(pl.multiple_of((2 * k + core) * own, 64), own), :] = same_ref[k]
        left_ref[pl.ds(pl.multiple_of((2 * k + 1 - core) * own, 64), own), :] = other_ref[k]
    sq_ref[...] = squares(left_ref[...])
    widen(mass_ref[...] - 0.5 * sq_ref[...], wide_ref)
    spread(out_ref, sampled_pass(left_ref, right_ref, wide_ref, shift_ref, total_ref))


def second_kernel(
    left_ref, right_ref, mass_ref, from_ref,
    out_ref, left_add_ref, right_add_ref, matrix_ref, wide_ref, shift_ref, total_ref,
):
    offset = 2.0 * mass_ref[...] - lse_over(planes(from_ref))
    left_add_ref[...] = offset
    widen(offset, wide_ref)
    spread(out_ref, sampled_pass(left_ref, right_ref, wide_ref, shift_ref, total_ref, matrix_ref))
    right_add_ref[...] = -shift_ref[...]


def close_pass(left_ref, right_ref, offset, fits, add_ref, wide_ref, shift_ref, total_ref, mean_ref=None):
    shift_ref[...] = -add_ref[...]
    totals = total_ref[...]

    @pl.when(jnp.logical_not(fits & (jnp.min(totals) > LOW) & (jnp.max(totals) < HIGH)))
    def _():
        widen(offset, wide_ref)
        exact_pass(left_ref, right_ref, wide_ref, shift_ref, total_ref, mean_ref)


def col_kernel(
    matrix_ref, obs_ref, gen_ref, mass_ref, from_ref, first_ref, obs_add_ref, gen_add_ref,
    out_ref, wide_ref, shift_ref, total_ref,
):
    offset = 2.0 * mass_ref[...] - lse_over(planes(from_ref))
    gain = offset - gen_add_ref[...]
    level = offset + first_ref[0]
    factors = jnp.exp(gain)
    for block in range(obs_ref.shape[0] // LANES):
        rows = pl.ds(block * LANES, LANES)
        total = jnp.zeros((LANES, LANES), jnp.float32)
        for part in range(gain.shape[0]):
            values = matrix_ref[rows, part * LANES : (part + 1) * LANES].astype(jnp.float32)
            total += values * factors[part : part + 1, :]
        total_ref[block : block + 1, :] = jnp.sum(jnp.transpose(total), axis=0, keepdims=True)
    lost = jnp.max(jnp.where(gain < -FAINT, level, -3e38))
    fits = (jnp.max(level) < STEEP) & (lost < -NOTHING)
    close_pass(gen_ref, obs_ref, offset, fits, obs_add_ref, wide_ref, shift_ref, total_ref)
    spread(out_ref, shift_ref[...] + jnp.log(total_ref[...]))


def row_kernel(
    matrix_ref, obs_ref, gen_ref, mass_ref, from_ref, obs_add_ref, gen_add_ref,
    out_ref, wide_ref, shift_ref, total_ref,
):
    offset = 2.0 * mass_ref[...] - lse_over(planes(from_ref))
    gain = offset - obs_add_ref[...]
    total = jnp.dot(in_parts(row_of(jnp.exp(gain))), matrix_ref[...], preferred_element_type=jnp.float32)
    total_ref[...] = dense_of(jnp.sum(total[:8, :], axis=0, keepdims=True))
    close_pass(obs_ref, gen_ref, offset, mild(gain), gen_add_ref, wide_ref, shift_ref, total_ref)
    spread(out_ref, shift_ref[...] + jnp.log(total_ref[...]))


def mild(gain):
    return (jnp.max(gain) < STEEP) & (jnp.min(gain) > -FAINT)


def mean_kernel(
    core_ref, matrix_ref, left_ref, right_ref, mass_ref, from_ref, left_add_ref, right_add_ref,
    out_ref, keep_ref, send_ref, wide_ref, shift_ref, total_ref, mean_ref,
):
    offset = 2.0 * mass_ref[...] - lse_over(planes(from_ref))
    gain = offset - left_add_ref[...]
    weight = row_of(jnp.exp(gain))
    left_t = jnp.transpose(left_ref[...].astype(jnp.float32)) * weight
    high = left_t.astype(jnp.bfloat16)
    low = (left_t - high.astype(jnp.float32)).astype(jnp.bfloat16)
    factors = jnp.concatenate([high, low, in_parts(weight)], axis=0)
    for chunk in range(right_ref.shape[0] // CHUNK):
        across = pl.ds(chunk * CHUNK, CHUNK)
        sums = jnp.dot(factors, matrix_ref[:, across], preferred_element_type=jnp.float32)
        total = jnp.sum(sums[2 * LANES : 2 * LANES + 8, :], axis=0, keepdims=True)
        store_row(total_ref, chunk * CHUNK // LANES, total)
        mean_ref[across, :] = jnp.transpose((sums[:LANES, :] + sums[LANES : 2 * LANES, :]) / total)
    close_pass(left_ref, right_ref, offset, mild(gain), right_add_ref, wide_ref, shift_ref, total_ref, mean_ref)
    out_ref[...] = shift_ref[...] + jnp.log(total_ref[...])
    core = core_ref[0]
    count, own, _ = keep_ref.shape
    for k in range(count):
        keep_ref[k] = mean_ref[pl.ds(pl.multiple_of((2 * k + core) * own, 64), own), :]
        send_ref[k] = mean_ref[pl.ds(pl.multiple_of((2 * k + 1 - core) * own, 64), own), :]


def pair_kernel(core_ref, keep_ref, came_ref, lse_ref, came_lse_ref, out_ref, wide_ref):
    core = core_ref[0]
    count, own, _ = keep_ref.shape
    both = lse_over([lse_ref[...], came_lse_ref[...]])
    widen(jnp.exp(lse_ref[...] - both), wide_ref)
    for k in range(count):
        share = wide_ref[pl.ds(pl.multiple_of((2 * k + core) * own, 64), own), :]
        out_ref[k, :own, :] = came_ref[k] + share * (keep_ref[k] - came_ref[k])
        out_ref[k, own:, :] = both


def last_kernel(col_ref, all_ref, points_ref, mass_ref, sq_ref, gen_ref, costate_ref, share_ref, wide_ref):
    own = points_ref.shape[0]
    count = all_ref.shape[0]
    parts = [all_ref[k, own:, :] for k in range(count)]
    total = lse_over(parts)
    gen_ref[...] = 2.0 * mass_ref[...] + sq_ref[...] - 2.0 * total
    first = col_ref[0] * own
    line = first // LANES
    inside = pl.multiple_of(first - line * LANES, 64)
    result = points_ref[...].astype(jnp.float32)
    span = wide_ref.shape[1] // LANES
    for k in range(count):
        share_ref[k] = jnp.exp(parts[k] - total)
        for part in range(span):
            row = jnp.broadcast_to(share_ref[k, pl.ds(line + part, 1), :], (LANES, LANES))
            wide_ref[k, part * LANES : (part + 1) * LANES, :] = jnp.transpose(row)
        result -= wide_ref[k, pl.ds(inside, own), :] * all_ref[k, :own, :]
    costate_ref[...] = result


def call(kernel, ins, outs, scratch, flops=0, exps=0):
    moved = sum(math.prod(x.shape) * x.dtype.itemsize for x in list(ins) + list(outs))
    return pl.pallas_call(
        kernel,
        out_shape=outs,
        in_specs=[SMEM if x.dtype == jnp.int32 else VMEM for x in ins],
        out_specs=[VMEM] * len(outs),
        scratch_shapes=scratch,
        compiler_params=pltpu.CompilerParams(vmem_limit_bytes=28 * 2**20),
        cost_estimate=pl.CostEstimate(flops=flops, bytes_accessed=moved, transcendentals=exps),
    )(*ins)


def f32(*shape):
    return jax.ShapeDtypeStruct(shape, jnp.float32)


def wide_scratch(n):
    return pltpu.VMEM((n, LANES), jnp.float32)


def body(n_row, n_col, points_gen, points_obs, log_mass_gen, log_mass_obs):
    own = points_gen.shape[0]
    half = n_col // 2
    groups = [list(range(core, n_col, 2)) for core in range(2)]
    pair = [(k, k ^ 1) for k in range(n_col)]
    col = lax.axis_index("col").astype(jnp.int32)
    core = lax.rem(col, 2).reshape(1)
    n, m = own * n_col, points_obs.shape[0] * n_row
    lines, obs_lines = n // LANES, m // LANES

    def over_row(blocks):
        return lax.all_to_all(blocks, "row", 0, 0)

    def over_col(blocks):
        return lax.all_to_all(blocks, "col", 0, 0)

    def over_chips(blocks):
        return lax.all_to_all(blocks, "col", 0, 0, axis_index_groups=groups)

    same = over_chips(jnp.broadcast_to(points_gen[None], (half,) + points_gen.shape))
    obs = over_row(jnp.broadcast_to(points_obs[None], (n_row,) + points_obs.shape)).reshape(m, LANES)
    other = lax.ppermute(same, "col", pair)
    mass_gen = log_mass_gen.reshape(lines, LANES)
    mass_obs = log_mass_obs.reshape(obs_lines, LANES)

    cost = dict(flops=2 * n * m * LANES, exps=n * m)
    product_cost = dict(flops=2 * n * m * LANES)
    small, gen_small = wide_scratch(obs_lines), wide_scratch(lines)
    col_out, row_out = f32(n_row, obs_lines, LANES), f32(n_col, lines, LANES)
    col_own, gen, gen_sq, obs_sq = call(
        first_kernel,
        (core, same, other, obs, mass_gen),
        [
            col_out,
            jax.ShapeDtypeStruct((n, LANES), points_gen.dtype),
            f32(lines, LANES),
            f32(obs_lines, LANES),
        ],
        [wide_scratch(n), small, small],
        **cost,
    )
    col_all = over_row(col_own)
    row_own, obs_add, gen_add, matrix = call(
        second_kernel,
        (obs, gen, mass_obs, col_all),
        [row_out, f32(obs_lines, LANES), f32(lines, LANES), jax.ShapeDtypeStruct((m, n), jnp.bfloat16)],
        [wide_scratch(m), gen_small, gen_small],
        **cost,
    )
    row_all = over_col(row_own)
    first = row_own
    for step in range(1, ITERS):
        (col_own,) = call(
            col_kernel,
            (matrix, obs, gen, mass_gen, row_all, first, obs_add, gen_add),
            [col_out],
            [wide_scratch(n), small, small],
            **product_cost,
        )
        col_all = over_row(col_own)
        if step == ITERS - 1:
            break
        (row_own,) = call(
            row_kernel,
            (matrix, obs, gen, mass_obs, col_all, obs_add, gen_add),
            [row_out],
            [wide_scratch(m), gen_small, gen_small],
            **product_cost,
        )
        row_all = over_col(row_own)
    row_lse, keep, send = call(
        mean_kernel,
        (core, matrix, obs, gen, mass_obs, col_all, obs_add, gen_add),
        [f32(lines, LANES), f32(half, own, LANES), f32(half, own, LANES)],
        [wide_scratch(m), gen_small, gen_small, wide_scratch(n)],
        **product_cost,
    )
    came = lax.ppermute(send, "col", pair)
    came_lse = lax.ppermute(row_lse, "col", pair)
    (joined,) = call(
        pair_kernel, (core, keep, came, row_lse, came_lse), [f32(half, own + lines, LANES)], [wide_scratch(n)]
    )
    joined_all = over_chips(joined)
    span = own // LANES + 1
    potential_gen, costate = call(
        last_kernel,
        (col.reshape(1), joined_all, points_gen, mass_gen, gen_sq),
        [f32(lines, LANES), f32(own, LANES)],
        [pltpu.VMEM((half, lines, LANES), jnp.float32), pltpu.VMEM((half, span * LANES, LANES), jnp.float32)],
    )
    potential_obs = 2.0 * mass_obs + obs_sq - 2.0 * lse_over([col_all[k] for k in range(n_row)])
    return potential_gen.reshape(-1), potential_obs.reshape(-1), costate


def solution(mesh):
    return jax.shard_map(
        functools.partial(body, mesh.shape["row"], mesh.shape["col"]),
        mesh=mesh,
        in_specs=(P(("row", "col"), None), P(("col", "row"), None), P("row"), P("col")),
        out_specs=(P("row"), P("col"), P(("row", "col"), None)),
        check_vma=False,
    )
```

time: 844 us -> 196 us (0.23)
  blocking collectives: 714 us -> 112 us
  other arithmetic: 98.2 us -> 0.63 us
  Pallas kernels: 0 us -> 45.2 us
  waiting for transfers between devices: 0.02 us -> 23.6 us
  matrix products: 15.7 us -> 0 us
  between operations: 14.2 us -> 0.74 us
  starting transfers between devices: 0.04 us -> 9.48 us
    pmax x8 -> x0, blocking collectives: 333 us -> none  [the longest x4 260 us: row_stats(): top = lax.pmax(jnp.max(row_scores, axis=1), 'col')]
    psum x8 -> x0, blocking collectives: 324 us -> none  [the longest x4 260 us: row_stats(): total = lax.psum(jnp.sum(jnp.exp(row_scores - top[:, None]), axis=1), 'col')]
    all_to_all x0 -> x8, blocking collectives: none -> 112 us  [the longest x4 60.3 us: over_row(): return lax.all_to_all(blocks, 'row', 0, 0)]
    all_gather x2 -> x0, blocking collectives: 57.2 us -> none  [the longest x1 30.4 us: body(): obs_block = lax.all_gather(points_obs, 'row', axis=0, tiled=True)]
    reduce_sum x10 -> x0, other arithmetic: 53.2 us -> none  [the longest x4 26.6 us: row_stats(): total = lax.psum(jnp.sum(jnp.exp(row_scores - top[:, None]), axis=1), 'col')]
    pallas_call x0 -> x10, Pallas kernels: none -> 45.2 us  [call(): pl.pallas_call(kernel, out_shape=outs, in_specs=[SMEM if x.dtype == jnp.i...]
    reduce_max x7 -> x0, other arithmetic: 42.7 us -> none  [the longest x4 25.3 us: row_stats(): top = lax.pmax(jnp.max(row_scores, axis=1), 'col')]
    all_to_all x0 -> x2, waiting for transfers between devices: none -> 21.8 us  [the longest x1 13.8 us: over_chips(): return lax.all_to_all(blocks, 'col', 0, 0, axis_index_groups=groups)]
  transfers between devices with their start and end apart: 1 -> 5, of which waited for: 0 -> 3; matrix products, arithmetic and copies ran while one was open for 1% -> 1% of each run, Pallas kernels for 0% -> 0%
where the time goes in v1:
time: 196 us; the launch traced here: 195 us
  blocking collectives  112 us (57%)
  Pallas kernels  45.2 us (23%)
  waiting for transfers between devices  23.6 us (12%)
  starting transfers between devices  9.48 us (5%)
  local copies, waits for them, and re-layouts  3.08 us (2%)
    all_to_all x4, blocking collectives, over_row(): return lax.all_to_all(blocks, 'row', 0, 0)  60.3 us
    pallas_call x10, Pallas kernels, call(): pl.pallas_call(kernel, out_shape=outs, in_specs=[SMEM if x.dtype == jnp.i...  45.2 us
    all_to_all x3, blocking collectives, over_col(): return lax.all_to_all(blocks, 'col', 0, 0)  35.1 us
    all_to_all x1, blocking collectives, over_chips(): return lax.all_to_all(blocks, 'col', 0, 0, axis_index_groups=groups)  17 us
    all_to_all x1, waiting for transfers between devices, over_chips(): return lax.all_to_all(blocks, 'col', 0, 0, axis_index_groups=groups)  13.8 us
    all_to_all x1, waiting for transfers between devices, over_row(): return lax.all_to_all(blocks, 'row', 0, 0)  7.94 us
    all_to_all x1, starting transfers between devices, over_row(): return lax.all_to_all(blocks, 'row', 0, 0)  5.34 us
  transfers between devices with their start and end apart: 5, of which 3 were waited for; matrix products, arithmetic and copies ran while one was open for 1% of the time, Pallas kernels for 0%

profile of v1, /device:TPU:0, one launch (start us, length us, event | category | flops | bytes accessed | tf_op | source)
XLA Modules:
  0.0 195.0 jit_solution(8905903257923638395)
XLA Ops:
  0.6 0.9 broadcast_in_dim.5
  1.5 17.0 %all_to_all.50.same_ref = bf16[8,192,128]{2,1,0:T(8,128)(2,1)S(1)} all-to-all(bf16[8,192,128]{2,1,0:T(8,128)(2,1)S(1)} %broadcast_in_dim.5), channel_id=1, replica_groups={{0,2,4,6,8,10,12,14},{1,3,5,7,9,11,13,15},{16,18,20,22,24,26,28,30},{17..., dimensions={0} | all-to-all | bytes 786432 | tf_op jit(solution)/shard_map/all_to_all | solution.py:317
  18.5 1.5 broadcast_in_dim.4
  20.0 5.3 %all-to-all-start = ((bf16[8,128,128]{2,1,0:T(8,128)(2,1)}), bf16[8,128,128]{2,1,0:T(8,128)(2,1)S(1)}, u32[]{:S(2)}, u32[]{:S(2)}) async-start(bf16[8,128,128]{2,1,0:T(8,128)(2,1)} %broadcast_in_dim.4), calls=%async_computation | async-start | bytes 524288 | tf_op jit(solution)/shard_map/all_to_all | solution.py:311
  25.3 7.9 %all-to-all-done = bf16[8,128,128]{2,1,0:T(8,128)(2,1)S(1)} async-done(((bf16[8,128,128]{2,1,0:T(8,128)(2,1)}), bf16[8,128,128]{2,1,0:T(8,128)(2,1)S(1)}, u32[]{:S(2)}, u32[]{:S(2)}) %all-to-all-start) | async-done | bytes 262176 | tf_op jit(solution)/shard_map/all_to_all | solution.py:311
  33.3 0.7 copy-done
  34.0 3.1 %shard_map.67 = (f32[8,8,128]{2,1,0:T(8,128)S(1)}, bf16[3072,128]{1,0:T(8,128)(2,1)S(1)}, f32[24,128]{1,0:T(8,128)S(1)}, f32[8,128]{1,0:T(8,128)S(1)}) custom-call(s32[1]{0:T(128)} %bitcast.1.core_ref, bf16[8,192,128]{2,1,0:T(8,128)(2,1)S(1)} %all_to_all.50.same_ref, bf16[8,192,128]{2,1,0:T(8,128)(2,1)S(1)} %collective-permute-done.other_ref, ...), custom_call_target="tpu_custom_call" | custom-call | flops 805306368 | bytes 1896452 | tf_op jit(solution)/shard_map/pallas_call | solution.py:281
  37.1 8.8 %all_to_all.51.from_ref = f32[8,8,128]{2,1,0:T(8,128)S(1)} all-to-all(f32[8,8,128]{2,1,0:T(8,128)S(1)} %get-tuple-element.17), channel_id=1, replica_groups=mesh['row'=8,'col'=16] {'row'}, dimensions={0} | all-to-all | bytes 65536 | tf_op jit(solution)/shard_map/all_to_all | solution.py:311
  45.9 17.6 %shard_map.68 = (f32[16,24,128]{2,1,0:T(8,128)S(1)}, f32[8,128]{1,0:T(8,128)S(1)}, f32[24,128]{1,0:T(8,128)S(1)}, bf16[1024,3072]{1,0:T(8,128)(2,1)S(1)}) custom-call(bf16[1024,128]{1,0:T(8,128)(2,1)S(1)} %bitcast.42, bf16[3072,128]{1,0:T(8,128)(2,1)S(1)} %get-tuple-element.16.right_ref.gen_ref, f32[8,128]{1,0:T(8,128)S(1)} %bitcast.54, ...), custom_call_target="tpu_custom_call" | custom-call | flops 805306368 | bytes 7589888 | tf_op jit(solution)/shard_map/pallas_call | solution.py:281
  63.5 12.1 %all_to_all.52.from_ref = f32[16,24,128]{2,1,0:T(8,128)S(1)} all-to-all(f32[16,24,128]{2,1,0:T(8,128)S(1)} %get-tuple-element.19.first_ref), channel_id=1, replica_groups=mesh['row'=8,'col'=16] {'col'}, dimensions={0} | all-to-all | bytes 393216 | tf_op jit(solution)/shard_map/all_to_all | solution.py:314
  75.6 1.5 shard_map.69
  77.2 21.3 %all_to_all.53.from_ref = f32[8,8,128]{2,1,0:T(8,128)S(1)} all-to-all(f32[8,8,128]{2,1,0:T(8,128)S(1)} %shard_map.69), channel_id=1, replica_groups=mesh['row'=8,'col'=16] {'row'}, dimensions={0} | all-to-all | bytes 65536 | tf_op jit(solution)/shard_map/all_to_all | solution.py:311
  98.5 1.1 shard_map.70
  99.6 11.5 %all_to_all.54.from_ref = f32[16,24,128]{2,1,0:T(8,128)S(1)} all-to-all(f32[16,24,128]{2,1,0:T(8,128)S(1)} %shard_map.70), channel_id=1, replica_groups=mesh['row'=8,'col'=16] {'col'}, dimensions={0} | all-to-all | bytes 393216 | tf_op jit(solution)/shard_map/all_to_all | solution.py:314
  111.0 1.5 shard_map.71
  112.5 21.4 %all_to_all.55.from_ref = f32[8,8,128]{2,1,0:T(8,128)S(1)} all-to-all(f32[8,8,128]{2,1,0:T(8,128)S(1)} %shard_map.71), channel_id=1, replica_groups=mesh['row'=8,'col'=16] {'row'}, dimensions={0} | all-to-all | bytes 65536 | tf_op jit(solution)/shard_map/all_to_all | solution.py:311
  133.9 1.1 shard_map.72
  135.1 11.5 %all_to_all.56.from_ref = f32[16,24,128]{2,1,0:T(8,128)S(1)} all-to-all(f32[16,24,128]{2,1,0:T(8,128)S(1)} %shard_map.72), channel_id=1, replica_groups=mesh['row'=8,'col'=16] {'col'}, dimensions={0} | all-to-all | bytes 393216 | tf_op jit(solution)/shard_map/all_to_all | solution.py:314
  146.5 14.3 %shard_map.73 = f32[8,8,128]{2,1,0:T(8,128)S(1)} custom-call(bf16[1024,3072]{1,0:T(8,128)(2,1)S(1)} %get-tuple-element.18.matrix_ref, bf16[1024,128]{1,0:T(8,128)(2,1)S(1)} %bitcast.47, bf16[3072,128]{1,0:T(8,128)(2,1)S(1)} %get-tuple-element.16.right_ref.gen_ref, f32[24,128]{1,0:T(8,128)S(1)} %bitcast.52, f32[16,24,128]{2,1,0:T(8,128)S(1)} %all_to_all.56.from_ref, ...), custom_call_target="tpu_custom_call" | custom-call | flops 805306368 | bytes 7794688 | tf_op jit(solution)/shard_map/pallas_call | solution.py:281
  160.8 0.0 copy-start.1
  160.8 0.0 copy-start.2
  160.9 8.8 %all_to_all.57.from_ref = f32[8,8,128]{2,1,0:T(8,128)S(1)} all-to-all(f32[8,8,128]{2,1,0:T(8,128)S(1)} %shard_map.73), channel_id=1, replica_groups=mesh['row'=8,'col'=16] {'row'}, dimensions={0} | all-to-all | bytes 65536 | tf_op jit(solution)/shard_map/all_to_all | solution.py:311
  169.6 2.3 %shard_map.74 = (f32[24,128]{1,0:T(8,128)S(1)}, f32[8,192,128]{2,1,0:T(8,128)S(1)}, f32[8,192,128]{2,1,0:T(8,128)S(1)}) custom-call(s32[1]{0:T(128)} %bitcast.1.core_ref, bf16[1024,3072]{1,0:T(8,128)(2,1)S(1)} %get-tuple-element.18.matrix_ref, bf16[1024,128]{1,0:T(8,128)(2,1)S(1)} %bitcast.48, bf16[3072,128]{1,0:T(8,128)(2,1)S(1)} %get-tuple-element.16.right_ref.gen_ref, ...), custom_call_target="tpu_custom_call" | custom-call | flops 805306368 | bytes 8978436 | tf_op jit(solution)/shard_map/pallas_call | solution.py:281
  171.9 0.1 collective-permute-start.1
  172.0 0.5 collective-permute-start.2
  172.5 1.8 collective-permute-done.2.came_lse_ref
  174.3 0.0 collective-permute-done.1.came_ref
  174.3 1.6 shard_map.75
  175.9 3.5 %all-to-all-start.9 = ((f32[8,216,128]{2,1,0:T(8,128)}), f32[8,216,128]{2,1,0:T(8,128)S(1)}, u32[]{:S(2)}, u32[]{:S(2)}) async-start(f32[8,216,128]{2,1,0:T(8,128)} %shard_map.75), calls=%async_computation.9 | async-start | bytes 1769472 | tf_op jit(solution)/shard_map/all_to_all | solution.py:317
  179.4 0.6 subtract_bitcast_fusion
  180.1 13.8 %all-to-all-done.9.all_ref = f32[8,216,128]{2,1,0:T(8,128)S(1)} async-done(((f32[8,216,128]{2,1,0:T(8,128)}), f32[8,216,128]{2,1,0:T(8,128)S(1)}, u32[]{:S(2)}, u32[]{:S(2)}) %all-to-all-start.9) | async-done | bytes 884768 | tf_op jit(solution)/shard_map/all_to_all | solution.py:317
  193.9 1.1 shard_map.76
  (7 shorter events, 0.0 us)
Async XLA Ops:
  0.6 45.2 %copy-start.3 = (f32[1024]{0:T(1024)S(1)}, f32[1024]{0:T(1024)}, u32[]{:S(2)}) copy-start(f32[1024]{0:T(1024)} %param.7) | copy-start | bytes 12292
  18.5 14.8 %collective-permute-start = (bf16[8,192,128]{2,1,0:T(8,128)(2,1)S(1)}, bf16[8,192,128]{2,1,0:T(8,128)(2,1)S(1)}, u32[]{:S(2)}, u32[]{:S(2)}) collective-permute-start(bf16[8,192,128]{2,1,0:T(8,128)(2,1)S(1)} %all_to_all.50.same_ref), channel_id=1, source_target_pairs={{0,1},{1,0},{2,3},{3,2},{4,5},{5,4},{6,7},{7,6},{8,9},{9,8},{10,11... | collective-permute-start | bytes 1179656 | tf_op jit(solution)/shard_map/ppermute | solution.py:321
  20.0 13.3 %all-to-all-start = ((bf16[8,128,128]{2,1,0:T(8,128)(2,1)}), bf16[8,128,128]{2,1,0:T(8,128)(2,1)S(1)}, u32[]{:S(2)}, u32[]{:S(2)}) async-start(bf16[8,128,128]{2,1,0:T(8,128)(2,1)} %broadcast_in_dim.4), calls=%async_computation | async-start | bytes 524288 | tf_op jit(solution)/shard_map/all_to_all | solution.py:311
  33.3 0.7 copy-start
  160.8 33.1 %copy-start.1 = (f32[3072]{0:T(1024)S(1)}, f32[3072]{0:T(1024)}, u32[]{:S(2)}) copy-start(f32[3072]{0:T(1024)} %param.6) | copy-start | bytes 36868
  160.8 33.1 %copy-start.2 = (bf16[192,128]{1,0:T(8,128)(2,1)S(1)}, bf16[192,128]{1,0:T(8,128)(2,1)}, u32[]{:S(2)}) copy-start(bf16[192,128]{1,0:T(8,128)(2,1)} %points_ref.1) | copy-start | bytes 147460
  171.9 2.4 %collective-permute-start.1 = (f32[8,192,128]{2,1,0:T(8,128)S(1)}, f32[8,192,128]{2,1,0:T(8,128)S(1)}, u32[]{:S(2)}, u32[]{:S(2)}) collective-permute-start(f32[8,192,128]{2,1,0:T(8,128)S(1)} %get-tuple-element.23), channel_id=1, source_target_pairs={{0,1},{1,0},{2,3},{3,2},{4,5},{5,4},{6,7},{7,6},{8,9},{9,8},{10,11... | collective-permute-start | bytes 2359304 | tf_op jit(solution)/shard_map/ppermute | solution.py:377
  172.0 2.3 %collective-permute-start.2 = (f32[24,128]{1,0:T(8,128)S(1)}, f32[24,128]{1,0:T(8,128)S(1)}, u32[]{:S(2)}, u32[]{:S(2)}) collective-permute-start(f32[24,128]{1,0:T(8,128)S(1)} %get-tuple-element.24.lse_ref), channel_id=1, source_target_pairs={{0,1},{1,0},{2,3},{3,2},{4,5},{5,4},{6,7},{7,6},{8,9},{9,8},{10,11... | collective-permute-start | bytes 36872 | tf_op jit(solution)/shard_map/ppermute | solution.py:378
  175.9 18.0 %all-to-all-start.9 = ((f32[8,216,128]{2,1,0:T(8,128)}), f32[8,216,128]{2,1,0:T(8,128)S(1)}, u32[]{:S(2)}, u32[]{:S(2)}) async-start(f32[8,216,128]{2,1,0:T(8,128)} %shard_map.75), calls=%async_computation.9 | async-start | bytes 1769472 | tf_op jit(solution)/shard_map/all_to_all | solution.py:317
